TPU v7x, 32 devices: a whole 2x2x4 slice. The times are simulated.
32 devices in a mesh: group: 2 (over x), dp: 16 (over z, y, core).
Axes of the slice: x: 2, y: 2, z: 4, core: 2. Of those that a mesh axis runs over, the one named last changes fastest.
Arguments:
- tokens: bfloat16 [1024, 8192], P(('group', 'dp')), parts along dimension 0, may hold values from -6 to 6
- cotangent: bfloat16 [1024, 8192], P(('group', 'dp')), parts along dimension 0, may hold values from -6 to 6
- lengths: int32 [16], P('group'), parts along dimension 0, may hold values from 16 to 64, as said below
- gate_weight: bfloat16 [8192, 28672], P(None, 'dp'), may hold values from -0.0625 to 0.0625
- up_weight: bfloat16 [8192, 28672], P(None, 'dp'), may hold values from -0.0625 to 0.0625
- down_weight: bfloat16 [28672, 8192], P('dp'), may hold values from -0.0625 to 0.0625
- proj_input: bfloat16 [8192, 64], replicated, may hold values from -0.0625 to 0.0625
- proj_cotangent: bfloat16 [8192, 64], replicated, may hold values from -0.0625 to 0.0625
- proj_hidden: bfloat16 [28672, 64], P('dp'), may hold values from -0.03125 to 0.03125
- proj_up: bfloat16 [28672, 64], P('dp'), may hold values from -0.03125 to 0.03125
- proj_gate: bfloat16 [28672, 64], P('dp'), may hold values from -0.03125 to 0.03125
- queries: float32 [32, 12288], P('group', 'dp'), parts along dimension 0, may hold values from -0.0546875 to 0.0546875
Outputs:
- logged: float32 [16, 12288], P('group', 'dp'), parts along dimension 0
- scores: float32 [32, 8], P('group'), parts along dimension 0
There are 2 independent parts, one for each index of `group`. A program takes and returns all parts, laid end to end along the dimension named above; an argument that names none is the same for every part. Nothing has to cross between parts.
Inputs may be any that keep to these rules, and one draw needn't show every extreme that they name: `lengths`: some sequence has exactly 64 live tokens and some exactly 16.
All inputs are finite; a program needn't handle non-finite values.
Results may differ from a plain program's by a relative error of at most 0.0031.
Values may be sent and summed in bfloat16 or wider, within the bound.
No kernel may reach another device: no remote copies, remote signals or barrier semaphores. Data moves between devices by JAX's collectives and lax.ppermute only.
A program may use at most 256 MiB of HBM per device.

v0:
```python
import math

import jax
import jax.numpy as jnp
from jax import lax
from jax.sharding import PartitionSpec as P

RANK = 64
LEN = 64
SEQS = 8


def silu_parts(gate):
    sigma = jax.nn.sigmoid(gate)
    return (gate * sigma, sigma * (1.0 + gate * (1.0 - sigma)))


def block_sketch(weight_rows, out_proj, in_proj):
    out_blocks = out_proj.reshape(SEQS, LEN, RANK)
    in_blocks = in_proj.reshape(SEQS, LEN, RANK)
    sketch = jnp.einsum(
        "sl,slo,sli->soi", weight_rows, out_blocks, in_blocks, precision=lax.Precision.HIGHEST
    )
    return sketch.reshape(SEQS, RANK * RANK)


def on_device(
    tokens,
    cotangent,
    lengths,
    gate_weight,
    up_weight,
    down_weight,
    proj_input,
    proj_cotangent,
    proj_hidden,
    proj_up,
    proj_gate,
    queries,
):
    scale = 1.0 / math.sqrt(LEN)
    hidden_cols = gate_weight.shape[1]
    piece = lax.all_gather(tokens, "dp", axis=0, tiled=True)
    forward = jnp.concatenate(
        [
            jnp.dot(piece, gate_weight, preferred_element_type=jnp.float32),
            jnp.dot(piece, up_weight, preferred_element_type=jnp.float32),
            jnp.dot(piece, proj_input, preferred_element_type=jnp.float32),
        ],
        axis=1,
    )
    gate = forward[:, :hidden_cols]
    up = forward[:, hidden_cols : 2 * hidden_cols]
    input_all = forward[:, 2 * hidden_cols :]
    silu_val, silu_grad = silu_parts(gate)
    hidden = (silu_val * up).astype(jnp.bfloat16)
    piece = lax.all_gather(cotangent, "dp", axis=0, tiled=True)
    back = lax.dot_general(
        piece, down_weight, (((1,), (1,)), ((), ())), preferred_element_type=jnp.float32
    )
    backward = jnp.concatenate(
        [back, jnp.dot(piece, proj_cotangent, preferred_element_type=jnp.float32)], axis=1
    )
    dhidden = backward[:, :hidden_cols]
    cot_all = backward[:, hidden_cols:]
    d_up = (dhidden * silu_val).astype(jnp.bfloat16)
    d_gate = (dhidden * up * silu_grad).astype(jnp.bfloat16)
    p_hid = jnp.dot(hidden, proj_hidden, preferred_element_type=jnp.float32)
    p_up = jnp.dot(d_up, proj_up, preferred_element_type=jnp.float32)
    p_gate = jnp.dot(d_gate, proj_gate, preferred_element_type=jnp.float32)
    a_hid, a_up, a_gate = lax.psum((p_hid, p_up, p_gate), "dp")
    live = (lax.iota(jnp.int32, LEN)[None, :] < lengths[:, None]).astype(jnp.float32) * scale
    logged = jnp.concatenate(
        [
            block_sketch(live, a_gate, input_all),
            block_sketch(live, a_up, input_all),
            block_sketch(live, cot_all, a_hid),
        ],
        axis=1,
    )
    width = queries.shape[1]
    logged_part = lax.dynamic_slice_in_dim(logged, lax.axis_index("dp") * width, width, 1)
    highest = lax.Precision.HIGHEST
    full_queries = lax.all_gather(queries, "dp", axis=1, tiled=True)
    gram = jnp.dot(logged, logged.T, precision=highest)
    cross = jnp.dot(full_queries, logged.T, precision=highest)
    damping = jnp.trace(gram) / SEQS
    system = gram + damping * jnp.eye(SEQS, dtype=jnp.float32)
    factor = jnp.linalg.cholesky(system)
    solved = jax.scipy.linalg.cho_solve((factor, True), cross.T)
    scores = damping * solved.T
    return (logged_part, scores)


def solution(mesh):
    placed = (
        P(("group", "dp"), None),
        P(("group", "dp"), None),
        P("group"),
        P(None, "dp"),
        P(None, "dp"),
        P("dp", None),
        P(),
        P(),
        P("dp", None),
        P("dp", None),
        P("dp", None),
        P("group", "dp"),
    )
    return jax.shard_map(
        on_device,
        mesh=mesh,
        in_specs=placed,
        out_specs=(P("group", "dp"), P("group", None)),
        check_vma=False,
    )
```

profile of v0, /device:TPU:0, one launch (start us, length us, event | category | flops | bytes accessed | tf_op | source)
XLA Modules:
  0.0 323.3 jit_solution(2916557463506697682)
XLA Ops:
  7.2 0.0 copy-start
  7.2 0.0 all-gather.3.cloned.1.call-start
  7.2 0.7 all-gather.3.cloned.1.call-update
  7.9 0.0 all-gather.5.cloned.1.call-start
  8.0 0.7 all-gather.5.cloned.1.call-update
  8.7 0.0 all-reduce.3.cloned.1.call-start
  8.7 0.7 fusion.20
  9.4 27.6 %all_gather.11 = f32[16,12288]{1,0:T(8,128)S(1)} all-gather(f32[16,768]{1,0:T(8,128)} %param.23), channel_id=1, replica_groups=mesh['group'=2,'dp'=16] {'dp'}, dimensions={1}, use_global_device_ids=true | all-gather | bytes 835584 | tf_op jit(solution)/shard_map/all_gather | solution.py:84
  37.1 52.3 %all-gather.3.cloned.1.call-done = bf16[512,8192]{1,0:T(8,128)(2,1)} async-done(((bf16[32,8192]{1,0:T(8,128)(2,1)}), bf16[512,8192]{1,0:T(8,128)(2,1)}) %all-gather.3.cloned.1.call-update) | async-done | bytes 8388624 | tf_op jit(solution)/shard_map/all_gather | solution.py:57
  89.4 22.8 %fusion.24 = f32[512,1792]{1,0:T(8,128)} fusion(bf16[512,8192]{1,0:T(8,128)(2,1)} %all-gather.3.cloned.1.call-done, bf16[1792,8192]{1,0:T(8,128)(2,1)} %param.17), kind=kOutput, calls=%fused_computation.41 | convolution fusion | flops 15032385536 | bytes 41418752 | tf_op jit(solution)/shard_map/dot_general | solution.py:58
  112.2 0.0 copy-start.3
  112.2 52.6 %all-gather.5.cloned.1.call-done = bf16[512,8192]{1,0:T(8,128)(2,1)} async-done(((bf16[32,8192]{1,0:T(8,128)(2,1)}), bf16[512,8192]{1,0:T(8,128)(2,1)}) %all-gather.5.cloned.1.call-update) | async-done | bytes 8388624 | tf_op jit(solution)/shard_map/all_gather | solution.py:43
  164.7 0.0 copy-start.6
  164.7 21.1 %fusion.26 = f32[512,1792]{1,0:T(8,128)S(1)} fusion(bf16[512,8192]{1,0:T(8,128)(2,1)} %all-gather.5.cloned.1.call-done, bf16[8192,1792]{1,0:T(8,128)(2,1)} %param.15), kind=kOutput, calls=%fused_computation.43 | convolution fusion | flops 15032385536 | bytes 41418752 | tf_op jit(solution)/shard_map/dot_general | solution.py:46
  185.9 0.0 copy-done.3
  185.9 0.0 copy-done.6
  185.9 0.0 copy-start.2
  185.9 1.3 fusion.1
  187.2 2.1 copy-done.2
  189.3 0.0 copy-start.4
  189.3 19.1 %fusion.25 = f32[512,1792]{1,0:T(8,128)S(1)} fusion(bf16[512,8192]{1,0:T(8,128)(2,1)S(1)} %copy-done.2, bf16[8192,1792]{1,0:T(8,128)(2,1)} %param.16), kind=kOutput, calls=%fused_computation.42 | convolution fusion | flops 15032385536 | bytes 41418752 | tf_op jit(solution)/shard_map/dot_general | solution.py:47
  208.4 0.0 copy-done.4
  208.4 0.0 copy-start.5
  208.4 1.8 fusion.3
  210.2 0.0 copy-done.5
  210.2 1.8 fusion.2
  212.0 0.1 reshape.46
  212.1 0.7 copy.16
  212.8 0.1 reshape.43
  212.9 0.7 copy.14
  213.7 0.0 all-reduce.3.cloned.1.call-update
  213.7 0.0 copy-done
  213.7 0.0 copy-start.1
  213.7 5.8 %fusion.27 = f32[512,64]{1,0:T(8,128)S(1)} fusion(bf16[512,8192]{1,0:T(8,128)(2,1)} %all-gather.5.cloned.1.call-done, bf16[8192,64]{0,1:T(8,128)(2,1)S(1)} %copy-done), kind=kOutput, calls=%fused_computation.44 | convolution fusion | flops 536870912 | bytes 9568256 | tf_op jit(solution)/shard_map/reshape | solution.py:20
  219.5 0.0 copy-done.1
  219.5 6.1 %fusion.28 = f32[512,64]{0,1:T(8,128)S(1)} fusion(bf16[512,8192]{1,0:T(8,128)(2,1)} %all-gather.3.cloned.1.call-done, bf16[8192,64]{0,1:T(8,128)(2,1)S(1)} %copy-done.1), kind=kOutput, calls=%fused_computation.45 | convolution fusion | flops 536870912 | bytes 9568256 | tf_op jit(solution)/shard_map/dot_general | solution.py:62
  225.6 0.1 reshape.48
  225.8 79.0 %all-reduce.3.cloned.1.call-done = (f32[8,64,64]{1,2,0:T(8,128)}, f32[8,64,64]{1,2,0:T(8,128)}, f32[8,64,64]{2,1,0:T(8,128)}) async-done(((f32[8,64,64]{1,2,0:T(8,128)}, f32[8,64,64]{1,2,0:T(8,128)}, f32[8,64,64]{2,1,0:T(8,128)}), (f32[8,64,64]{1,2,0:T(8,128)}, f32[8,64,64]{1,2,0:T(8,128)}, f32[8,64,64]{2,1,0:T(8,128)})) %all-reduce.3.cloned.1.call-update) | async-done | bytes 393232 | tf_op jit(solution)/shard_map/psum | solution.py:71
  304.7 1.4 fusion.6
  306.1 0.1 reshape.50
  306.2 1.4 fusion.9
  307.6 1.4 fusion.7
  308.9 0.1 reshape.47
  309.0 0.1 reshape.45
  309.2 1.6 select_reduce_fusion.1
  310.8 1.0 fusion.29
  311.8 0.6 constant_dynamic-slice_fusion
  312.4 0.1 copy.20
  313.2 0.7 cholesky.13
  313.9 0.6 compare_reduce_fusion
  314.5 0.6 fusion.14
  315.2 0.6 custom-call.10
  315.8 0.2 fusion.16
  316.0 0.7 convolution_multiply_fusion
  (5 shorter events, 0.1 us)
Async XLA Ops:
  7.2 206.5 %copy-start = (bf16[8192,64]{0,1:T(8,128)(2,1)S(1)}, bf16[8192,64]{0,1:T(8,128)(2,1)}, u32[]{:S(2)}) copy-start(bf16[8192,64]{0,1:T(8,128)(2,1)} %param.18) | copy-start | bytes 3145732
  7.2 82.2 %all-gather.3.cloned.1.call-start = ((), (), s32[]{:S(2)}) async-start(), calls=%async_computation | async-start | bytes 8912896 | tf_op jit(solution)/shard_map/all_gather | solution.py:57
  7.9 156.8 %all-gather.5.cloned.1.call-start = ((), (), s32[]{:S(2)}) async-start(), calls=%async_computation.1 | async-start | bytes 8912896 | tf_op jit(solution)/shard_map/all_gather | solution.py:43
  8.7 296.1 %all-reduce.3.cloned.1.call-start = ((), (), s32[]{:S(2)}) async-start(), calls=%async_computation.2 | async-start | bytes 1572864 | tf_op jit(solution)/shard_map/psum | solution.py:71
  112.2 73.7 %copy-start.3 = (bf16[1792,64]{0,1:T(8,128)(2,1)S(1)}, bf16[1792,64]{0,1:T(8,128)(2,1)}, u32[]{:S(2)}) copy-start(bf16[1792,64]{0,1:T(8,128)(2,1)} %param.21) | copy-start | bytes 688132
  164.7 21.2 %copy-start.6 = (f32[512,1792]{1,0:T(8,128)S(1)}, f32[512,1792]{1,0:T(8,128)}, u32[]{:S(2)}) copy-start(f32[512,1792]{1,0:T(8,128)} %fusion.24) | copy-start | bytes 11010052
  185.9 3.4 %copy-start.2 = (bf16[512,8192]{1,0:T(8,128)(2,1)S(1)}, bf16[512,8192]{1,0:T(8,128)(2,1)}, u32[]{:S(2)}) copy-start(bf16[512,8192]{1,0:T(8,128)(2,1)} %all-gather.5.cloned.1.call-done) | copy-start | bytes 25165828
  189.3 19.1 %copy-start.4 = (bf16[1792,64]{0,1:T(8,128)(2,1)S(1)}, bf16[1792,64]{0,1:T(8,128)(2,1)}, u32[]{:S(2)}) copy-start(bf16[1792,64]{0,1:T(8,128)(2,1)} %param.22) | copy-start | bytes 688132
  208.4 1.8 copy-start.5
  213.7 5.8 %copy-start.1 = (bf16[8192,64]{0,1:T(8,128)(2,1)S(1)}, bf16[8192,64]{0,1:T(8,128)(2,1)}, u32[]{:S(2)}) copy-start(bf16[8192,64]{0,1:T(8,128)(2,1)} %param.19) | copy-start | bytes 3145732
Sparse Core Ops, SparseCore 0:
  10.2 79.1 all-gather.2
  91.5 73.1 all-gather.4
  213.8 90.8 all-reduce.2
where the time goes:
time: 324 us; the launch traced here: 323 us
  waiting for transfers between devices  185 us (57%)
  matrix products  87.3 us (27%)
  blocking collectives  27.6 us (9%)
  between operations  14.6 us (5%)
  local copies, waits for them, and re-layouts  5 us (2%)
  other arithmetic  3.4 us (1%)
    psum x1, waiting for transfers between devices, on_device(): a_hid, a_up, a_gate = lax.psum((p_hid, p_up, p_gate), 'dp')  79 us
    all_gather x1, waiting for transfers between devices, on_device(): piece = lax.all_gather(tokens, 'dp', axis=0, tiled=True)  52.6 us
    all_gather x1, waiting for transfers between devices, on_device(): piece = lax.all_gather(cotangent, 'dp', axis=0, tiled=True)  52.3 us
    all_gather x1, blocking collectives, on_device(): full_queries = lax.all_gather(queries, 'dp', axis=1, tiled=True)  27.6 us
    dot_general x1, matrix products, on_device(): lax.dot_general(piece, down_weight, (((1,), (1,)), ((), ())), preferred_e...  22.8 us
    dot_general x1, matrix products, on_device(): jnp.dot(piece, gate_weight, preferred_element_type=jnp.float32)  21.1 us
    dot_general x1, matrix products, on_device(): jnp.dot(piece, up_weight, preferred_element_type=jnp.float32)  19.1 us
    reshape x2, matrix products, block_sketch(): in_blocks = in_proj.reshape(SEQS, LEN, RANK)  7.56 us
  transfers between devices with their start and end apart: 3, of which 3 were waited for; matrix products, arithmetic and copies ran while one was open for 11% of the time, Pallas kernels for 0%

commit v1 on v0

v1 whole, which is shorter than its diff:
```python
import math

import jax
import jax.numpy as jnp
from jax import lax
from jax.experimental import pallas as pl
from jax.experimental.pallas import tpu as pltpu
from jax.sharding import PartitionSpec as P

RANK = 64
LEN = 64
SEQS = 8
HIGHEST = lax.Precision.HIGHEST
F32 = jnp.float32
BF16 = jnp.bfloat16


def silu_parts(gate):
    sigma = jax.nn.sigmoid(gate)
    return (gate * sigma, sigma * (1.0 + gate * (1.0 - sigma)))


def block_sketch(weight_rows, out_proj, in_proj):
    out_blocks = out_proj.reshape(SEQS, LEN, RANK)
    in_blocks = in_proj.reshape(SEQS, LEN, RANK)
    sketch = jnp.einsum(
        "sl,slo,sli->soi", weight_rows, out_blocks, in_blocks, precision=HIGHEST
    )
    return sketch.reshape(SEQS, RANK * RANK)


def on_device(
    tokens,
    cotangent,
    lengths,
    gate_weight,
    up_weight,
    down_weight,
    proj_input,
    proj_cotangent,
    proj_hidden,
    proj_up,
    proj_gate,
    queries,
):
    scale = 1.0 / math.sqrt(LEN)
    piece = lax.all_gather(tokens, "dp", axis=0, tiled=True)
    gate = jnp.dot(piece, gate_weight, preferred_element_type=F32)
    up = jnp.dot(piece, up_weight, preferred_element_type=F32)
    input_all = jnp.dot(piece, proj_input, preferred_element_type=F32)
    silu_val, silu_grad = silu_parts(gate)
    hidden = (silu_val * up).astype(BF16)
    piece = lax.all_gather(cotangent, "dp", axis=0, tiled=True)
    dhidden = lax.dot_general(
        piece, down_weight, (((1,), (1,)), ((), ())), preferred_element_type=F32
    )
    cot_all = jnp.dot(piece, proj_cotangent, preferred_element_type=F32)
    d_up = (dhidden * silu_val).astype(BF16)
    d_gate = (dhidden * up * silu_grad).astype(BF16)
    p_hid = jnp.dot(hidden, proj_hidden, preferred_element_type=F32)
    p_up = jnp.dot(d_up, proj_up, preferred_element_type=F32)
    p_gate = jnp.dot(d_gate, proj_gate, preferred_element_type=F32)
    a_hid, a_up, a_gate = lax.psum((p_hid, p_up, p_gate), "dp")
    live = (lax.iota(jnp.int32, LEN)[None, :] < lengths[:, None]).astype(F32) * scale
    logged = jnp.concatenate(
        [
            block_sketch(live, a_gate, input_all),
            block_sketch(live, a_up, input_all),
            block_sketch(live, cot_all, a_hid),
        ],
        axis=1,
    )
    width = queries.shape[1]
    logged_part = lax.dynamic_slice_in_dim(logged, lax.axis_index("dp") * width, width, 1)
    full_queries = lax.all_gather(queries, "dp", axis=1, tiled=True)
    gram = jnp.dot(logged, logged.T, precision=HIGHEST)
    cross = jnp.dot(full_queries, logged.T, precision=HIGHEST)
    damping = jnp.trace(gram) / SEQS
    system = gram + damping * jnp.eye(SEQS, dtype=F32)
    factor = jnp.linalg.cholesky(system)
    solved = jax.scipy.linalg.cho_solve((factor, True), cross.T)
    scores = damping * solved.T
    return (logged_part, scores)


PLACES = [(z, y, c) for z in range(4) for y in range(2) for c in range(2)]


def spot(z, y, c):
    return 4 * z + 2 * y + c


CORE = [(spot(z, y, c), spot(z, y, 1 - c)) for z, y, c in PLACES]
YSWAP = [(spot(z, y, c), spot(z, 1 - y, c)) for z, y, c in PLACES]
ZPAIR = [(spot(z, y, c), spot(z ^ 1, y, c)) for z, y, c in PLACES]
ZMID = [(spot(z, y, c), spot(3 - z, y, c)) for z, y, c in PLACES if z in (1, 2)]
ZOUT = [(spot(z, y, c), spot(z ^ 1, y, c)) for z, y, c in PLACES if z in (1, 2)]


def send(x, pairs):
    return lax.ppermute(x, "dp", pairs)


def send_z(x, targets):
    return send(x, [(spot(z, y, c), spot(targets[z], y, c)) for z, y, c in PLACES if z in targets])


def gather_near(x):
    half = x.shape[1] // 2
    from_z = send(x, ZPAIR)
    from_y = send(x, YSWAP)
    diag_z = send(from_y[:, :half], ZPAIR)
    diag_y = send(from_z[:, half:], YSWAP)
    diag = jnp.concatenate([diag_z, diag_y], axis=1)
    mine = jnp.concatenate([x, from_z, from_y, diag], axis=0)
    return mine, send(mine, CORE)


def gather_far(mine, z, y, parts):
    half = mine.shape[1] // 2
    step = half // parts
    rows = mine.shape[0] // 2
    turned = jnp.concatenate([mine[rows:, half:], mine[:rows, half:]], axis=0)
    share = jnp.where(y == 0, mine[:, :half], turned)
    pieces = []
    for part in range(parts):
        block = share[:, part * step : (part + 1) * step]
        middle = send(block, ZMID)
        outer = send(middle, ZOUT)
        got = jnp.where((z == 1) | (z == 2), middle, outer)
        other = send(got, YSWAP)
        low = jnp.where(y == 0, got, other)
        high = jnp.where(y == 0, other, got)
        both = jnp.concatenate([low, high], axis=1)
        both = jnp.concatenate([both, send(both, CORE)], axis=0)
        pieces.append(((part * step, step), both[:, :step]))
        pieces.append(((half + part * step, step), both[:, step:]))
    return pieces


def canonical(near, far, z, y, c):
    n = near.shape[1]
    near = near.reshape(2, 2, 2, 32, n)
    far = far.reshape(2, 2, 2, 32, n)
    near = jnp.where(z % 2 == 1, near[:, :, ::-1], near)
    near = jnp.where(y == 1, near[:, ::-1], near)
    far = jnp.where(z // 2 == 1, far[:, :, ::-1], far)
    both = jnp.stack([near, far])
    both = jnp.where(z // 2 == 1, both[::-1], both)
    both = jnp.where(c == 1, both[:, ::-1], both)
    both = both.transpose(0, 3, 2, 1, 4, 5)
    return both.reshape(512, n)


def dot_pieces(pieces, weight, axis):
    total = None
    for (start, size), block in pieces:
        part = lax.dot_general(
            block,
            lax.slice_in_dim(weight, start, start + size, axis=axis),
            (((1,), (axis,)), ((), ())),
            preferred_element_type=F32,
        )
        total = part if total is None else total + part
    return total


def dot(a, b):
    return jnp.dot(a, b, preferred_element_type=F32)


def sum_all(x):
    x = x + send(x, CORE)
    x = x + send(x, YSWAP)
    parts = [send_z(x, {z: (z + d) % 4 for z in range(4)}) for d in (1, 2, 3)]
    return (x + parts[1]) + (parts[0] + parts[2])


def solve_kernel(stats_ref, out_ref):
    stats = stats_ref[...]
    gram = stats[:SEQS]
    row = lax.broadcasted_iota(jnp.int32, (SEQS, SEQS), 0)
    col = lax.broadcasted_iota(jnp.int32, (SEQS, SEQS), 1)
    eye = (row == col).astype(F32)
    damping = jnp.sum(gram * eye) / SEQS
    left = gram + damping * eye
    right = eye
    for k in range(SEQS):
        pivot = left[k : k + 1, k : k + 1]
        left_row = left[k : k + 1, :] / pivot
        right_row = right[k : k + 1, :] / pivot
        factor = jnp.where(row[:, :1] == k, 0.0, left[:, k : k + 1])
        left = jnp.where(row == k, left_row, left - factor * left_row)
        right = jnp.where(row == k, right_row, right - factor * right_row)
    cross = stats[SEQS:]
    out_ref[...] = damping * jnp.dot(cross, right, precision=HIGHEST, preferred_element_type=F32)


def on_device_424(
    tokens,
    cotangent,
    lengths,
    gate_weight,
    up_weight,
    down_weight,
    proj_input,
    proj_cotangent,
    proj_hidden,
    proj_up,
    proj_gate,
    queries,
):
    index = lax.axis_index("dp")
    z, y, c = index // 4, (index // 2) % 2, index % 2
    far_parts = 2

    tok_mine, tok_other = gather_near(tokens)
    cot_mine, cot_other = gather_near(cotangent)
    tok_far = gather_far(tok_mine, z, y, far_parts)
    cot_far = gather_far(cot_mine, z, y, far_parts)

    tok_near = jnp.concatenate([tok_mine, tok_other], axis=0)
    gate_near = dot(tok_near, gate_weight)
    up_near = dot(tok_near, up_weight)
    cot_near = jnp.concatenate([cot_mine, cot_other], axis=0)
    dh_near = lax.dot_general(
        cot_near, down_weight, (((1,), (1,)), ((), ())), preferred_element_type=F32
    )
    gate_far = dot_pieces(tok_far, gate_weight, 0)
    up_far = dot_pieces(tok_far, up_weight, 0)
    dh_far = dot_pieces(cot_far, down_weight, 1)

    def layer(gate, up, dhidden):
        silu_val, silu_grad = silu_parts(gate)
        hidden = (silu_val * up).astype(BF16)
        d_up = (dhidden * silu_val).astype(BF16)
        d_gate = (dhidden * up * silu_grad).astype(BF16)
        return dot(hidden, proj_hidden), dot(d_gate, proj_gate), dot(d_up, proj_up)

    hid_near, pg_near, pu_near = layer(gate_near, up_near, dh_near)
    hid_far, pg_far, pu_far = layer(gate_far, up_far, dh_far)

    a_in = canonical(dot(tok_near, proj_input), dot_pieces(tok_far, proj_input, 0), z, y, c)
    a_cot = canonical(dot(cot_near, proj_cotangent), dot_pieces(cot_far, proj_cotangent, 0), z, y, c)
    a_hid = sum_all(canonical(hid_near, hid_far, z, y, c))

    p_near = jnp.concatenate([pg_near, pu_near], axis=1)
    p_far = jnp.concatenate([pg_far, pu_far], axis=1)
    p = canonical(p_near, p_far, z, y, c).T
    mine = 3 * RANK // 16
    slots = -(-2 * RANK // mine)
    slots = -(-slots // 4) * 4
    p = jnp.pad(p, ((0, slots * mine - 2 * RANK), (0, 0))).reshape(slots // 4, 2, 2, mine, -1)
    keep = jnp.where(c == 0, p[:, :, 0], p[:, :, 1])
    give = jnp.where(c == 0, p[:, :, 1], p[:, :, 0])
    p = keep + send(give, CORE)
    keep = jnp.where(y == 0, p[:, 0], p[:, 1])
    give = jnp.where(y == 0, p[:, 1], p[:, 0])
    p = keep + send(give, YSWAP)
    planes = slots // 4
    total = lax.dynamic_index_in_dim(p, jnp.minimum(z, planes - 1), 0, keepdims=False)
    for d in (1, 2, 3):
        target = lax.rem(z + d, 4)
        block = lax.dynamic_index_in_dim(p, jnp.minimum(target, planes - 1), 0, keepdims=False)
        total = total + send_z(block, {s: (s + d) % 4 for s in range(4) if (s + d) % 4 < planes})

    rows = index * mine + lax.iota(jnp.int32, mine)
    cot_rows = lax.dynamic_slice_in_dim(
        jnp.pad(a_cot.T, ((mine, 0), (0, 0))), jnp.maximum(index * mine - 2 * RANK + mine, 0), mine, 0
    )
    summed = rows < 2 * RANK
    out_rows = jnp.where(summed[:, None], total, cot_rows)
    scale = 1.0 / math.sqrt(LEN)
    live = (lax.iota(jnp.int32, LEN)[None, :] < lengths[:, None]).astype(F32) * scale
    owner = jnp.eye(SEQS, dtype=F32)
    weights = (owner[:, :, None] * live[None]).reshape(SEQS, SEQS * LEN)
    left = (weights[:, None, :] * out_rows[None]).reshape(SEQS * mine, -1)
    sketch = jnp.dot(left, jnp.concatenate([a_in, a_hid], axis=1), precision=HIGHEST)
    sketch = sketch.reshape(SEQS, mine, 2 * RANK)
    sketch = jnp.where(summed[None, :, None], sketch[:, :, :RANK], sketch[:, :, RANK:])
    logged = sketch.reshape(SEQS, mine * RANK)
    stats = jnp.dot(jnp.concatenate([logged, queries], axis=0), logged.T, precision=HIGHEST)
    stats = sum_all(stats)
    scores = pl.pallas_call(
        solve_kernel, out_shape=jax.ShapeDtypeStruct((queries.shape[0], SEQS), F32)
    )(stats)
    return (logged, scores)


def solution(mesh):
    placed = (
        P(("group", "dp"), None),
        P(("group", "dp"), None),
        P("group"),
        P(None, "dp"),
        P(None, "dp"),
        P("dp", None),
        P(),
        P(),
        P("dp", None),
        P("dp", None),
        P("dp", None),
        P("group", "dp"),
    )
    return jax.shard_map(
        on_device_424 if mesh.shape["dp"] == 16 else on_device,
        mesh=mesh,
        in_specs=placed,
        out_specs=(P("group", "dp"), P("group", None)),
        check_vma=False,
    )
```

time: 324 us -> 334 us (1.031); the launches traced: 323 us -> 328 us
  waiting for transfers between devices: 185 us -> 121 us
  starting transfers between devices: 0.11 us -> 44.5 us
  matrix products: 87.3 us -> 125 us
  blocking collectives: 27.6 us -> 0 us
  other arithmetic: 3.4 us -> 16.7 us
  between operations: 14.6 us -> 2.22 us
  local copies, waits for them, and re-layouts: 5 us -> 16.1 us
    ppermute x0 -> x41, waiting for transfers between devices: none -> 121 us  [send(): return lax.ppermute(x, 'dp', pairs)]
    all_gather x2 -> x0, waiting for transfers between devices: 105 us -> none  [the longest x1 52.6 us: on_device(): piece = lax.all_gather(tokens, 'dp', axis=0, tiled=True)]
    psum x1 -> x0, waiting for transfers between devices: 79 us -> none  [on_device(): a_hid, a_up, a_gate = lax.psum((p_hid, p_up, p_gate), 'dp')]
    dot_general x11 -> x33, matrix products: 78.8 us -> 125 us  [the longest x20 69.1 us: dot_pieces(): lax.dot_general(block, lax.slice_in_dim(weight, start, start + size, axis...]
    ppermute x0 -> x41, starting transfers between devices: none -> 44.5 us  [send(): return lax.ppermute(x, 'dp', pairs)]
    all_gather x1 -> x0, blocking collectives: 27.6 us -> none  [on_device(): full_queries = lax.all_gather(queries, 'dp', axis=1, tiled=True)]
    unnamed x16 -> x88, local copies, waits for them, and re-layouts: 2.14 us -> 12.9 us
    concatenate x0 -> x12, other arithmetic: none -> 10.2 us  [the longest x4 4.58 us: gather_far(): both = jnp.concatenate([low, high], axis=1)]
  transfers between devices with their start and end apart: 3 -> 41, of which waited for: 3 -> 19; matrix products, arithmetic and copies ran while one was open for 11% -> 37% of each run, Pallas kernels for 0% -> 0%
where the time goes in v1:
time: 334 us; the launch traced here: 328 us
  matrix products  125 us (37%)
  waiting for transfers between devices  121 us (36%)
  starting transfers between devices  44.5 us (13%)
  other arithmetic  16.7 us (5%)
  local copies, waits for them, and re-layouts  16.1 us (5%)
    ppermute x41, waiting for transfers between devices, send(): return lax.ppermute(x, 'dp', pairs)  121 us
    dot_general x20, matrix products, dot_pieces(): lax.dot_general(block, lax.slice_in_dim(weight, start, start + size, axis...  69.1 us
    ppermute x41, starting transfers between devices, send(): return lax.ppermute(x, 'dp', pairs)  44.5 us
    dot_general x10, matrix products, dot(): return jnp.dot(a, b, preferred_element_type=F32)  38.7 us
    dot_general x1, matrix products, on_device_424(): lax.dot_general(cot_near, down_weight, (((1,), (1,)), ((), ())), preferre...  16.3 us
    unnamed x88, local copies, waits for them, and re-layouts  12.9 us
  transfers between devices with their start and end apart: 41, of which 19 were waited for; matrix products, arithmetic and copies ran while one was open for 37% of the time, Pallas kernels for 0%

profile of v1, /device:TPU:0, one launch (start us, length us, event | category | flops | bytes accessed | tf_op | source)
XLA Modules:
  0.0 328.0 jit_solution(4358094122072274392)
XLA Ops:
  0.6 3.0 collective-permute-start.6
  3.7 1.6 collective-permute-start.5
  5.8 1.9 constant_dynamic-update-slice_fusion.13
  9.8 6.8 %collective-permute-done.6 = bf16[32,8192]{1,0:T(8,128)(2,1)S(1)} collective-permute-done((bf16[32,8192]{1,0:T(8,128)(2,1)}, bf16[32,8192]{1,0:T(8,128)(2,1)S(1)}, u32[]{:S(2)}, u32[]{:S(2)}) %collective-permute-start.6) | collective-permute-done | bytes 524320 | tf_op jit(solution)/shard_map/ppermute | solution.py:101
  16.7 2.2 collective-permute-start.7
  18.9 1.6 collective-permute-start.8
  20.5 7.4 %collective-permute-done.1 = bf16[32,8192]{1,0:T(8,128)(2,1)S(1)} collective-permute-done((bf16[32,8192]{1,0:T(8,128)(2,1)}, bf16[32,8192]{1,0:T(8,128)(2,1)S(1)}, u32[]{:S(2)}, u32[]{:S(2)}) %collective-permute-start.1) | collective-permute-done | bytes 524320 | tf_op jit(solution)/shard_map/ppermute | solution.py:101
  27.9 2.2 collective-permute-start.2
  30.1 1.6 collective-permute-start.3
  33.5 2.1 collective-permute-done.7
  37.5 1.2 copy-done.1
  40.6 1.9 copy-done.23
  44.8 1.5 collective-permute-start.10
  46.3 1.5 collective-permute-start.14
  47.8 1.3 collective-permute-start.19
  49.1 1.3 collective-permute-start.23
  51.1 1.3 collective-permute-start.11
  52.4 16.9 %collective-permute-done.19 = bf16[128,2048]{1,0:T(8,128)(2,1)} collective-permute-done((bf16[128,2048]{1,0:T(8,128)(2,1)S(1)}, bf16[128,2048]{1,0:T(8,128)(2,1)}, u32[]{:S(2)}, u32[]{:S(2)}) %collective-permute-start.19) | collective-permute-done | bytes 524320 | tf_op jit(solution)/shard_map/ppermute | solution.py:101
  69.4 1.3 collective-permute-start.15
  71.8 5.7 %collective-permute-done.23 = bf16[128,2048]{1,0:T(8,128)(2,1)} collective-permute-done((bf16[128,2048]{1,0:T(8,128)(2,1)S(1)}, bf16[128,2048]{1,0:T(8,128)(2,1)}, u32[]{:S(2)}, u32[]{:S(2)}) %collective-permute-start.23) | collective-permute-done | bytes 524320 | tf_op jit(solution)/shard_map/ppermute | solution.py:101
  79.1 22.4 %collective-permute-done.11 = bf16[128,2048]{1,0:T(8,128)(2,1)S(1)} collective-permute-done((bf16[128,2048]{1,0:T(8,128)(2,1)}, bf16[128,2048]{1,0:T(8,128)(2,1)S(1)}, u32[]{:S(2)}, u32[]{:S(2)}) %collective-permute-start.11) | collective-permute-done | bytes 524320 | tf_op jit(solution)/shard_map/ppermute | solution.py:101
  102.1 6.1 %collective-permute-done.15 = bf16[128,2048]{1,0:T(8,128)(2,1)S(1)} collective-permute-done((bf16[128,2048]{1,0:T(8,128)(2,1)}, bf16[128,2048]{1,0:T(8,128)(2,1)S(1)}, u32[]{:S(2)}, u32[]{:S(2)}) %collective-permute-start.15) | collective-permute-done | bytes 524320 | tf_op jit(solution)/shard_map/ppermute | solution.py:101
  108.8 1.6 collective-permute-start.16
  111.6 3.3 %collective-permute-done.24 = bf16[128,2048]{1,0:T(8,128)(2,1)S(1)} collective-permute-done((bf16[128,2048]{1,0:T(8,128)(2,1)S(1)}, bf16[128,2048]{1,0:T(8,128)(2,1)S(1)}, u32[]{:S(2)}, u32[]{:S(2)}) %collective-permute-start.24) | collective-permute-done | bytes 524320 | tf_op jit(solution)/shard_map/ppermute | solution.py:101
  116.2 10.0 %collective-permute-done.12 = bf16[128,2048]{1,0:T(8,128)(2,1)S(1)} collective-permute-done((bf16[128,2048]{1,0:T(8,128)(2,1)S(1)}, bf16[128,2048]{1,0:T(8,128)(2,1)S(1)}, u32[]{:S(2)}, u32[]{:S(2)}) %collective-permute-start.12) | collective-permute-done | bytes 524320 | tf_op jit(solution)/shard_map/ppermute | solution.py:101
  126.3 1.2 pad_maximum_fusion.10
  127.4 5.7 %collective-permute-done.16 = bf16[128,2048]{1,0:T(8,128)(2,1)S(1)} collective-permute-done((bf16[128,2048]{1,0:T(8,128)(2,1)S(1)}, bf16[128,2048]{1,0:T(8,128)(2,1)S(1)}, u32[]{:S(2)}, u32[]{:S(2)}) %collective-permute-start.16) | collective-permute-done | bytes 524320 | tf_op jit(solution)/shard_map/ppermute | solution.py:101
  135.1 13.6 %fusion.147 = f32[256,1792]{1,0:T(8,128)S(1)} fusion(bf16[256,8192]{1,0:T(8,128)(2,1)S(1)} %constant_dynamic-update-slice_fusion.9, bf16[8192,1792]{1,0:T(8,128)(2,1)} %param.15), kind=kOutput, calls=%fused_computation.222 | convolution fusion | flops 7516192768 | bytes 35389440 | tf_op jit(solution)/shard_map/dot_general | solution.py:169
  148.7 13.5 %fusion.146 = f32[256,1792]{1,0:T(8,128)S(1)} fusion(bf16[256,8192]{1,0:T(8,128)(2,1)S(1)} %constant_dynamic-update-slice_fusion.9, bf16[8192,1792]{1,0:T(8,128)(2,1)} %param.16), kind=kOutput, calls=%fused_computation.221 | convolution fusion | flops 7516192768 | bytes 35389440 | tf_op jit(solution)/shard_map/dot_general | solution.py:169
  162.2 1.2 fusion.149
  165.9 16.3 %fusion.145 = f32[256,1792]{1,0:T(8,128)} fusion(bf16[256,8192]{1,0:T(8,128)(2,1)S(1)} %constant_dynamic-update-slice_fusion.2, bf16[1792,8192]{1,0:T(8,128)(2,1)} %param.17), kind=kOutput, calls=%fused_computation.220 | convolution fusion | flops 7516192768 | bytes 35389440 | tf_op jit(solution)/shard_map/dot_general | solution.py:226
  182.2 2.5 fusion.76
  186.2 3.8 %fusion.148 = f32[256,64]{1,0:T(8,128)S(1)} fusion(bf16[256,8192]{1,0:T(8,128)(2,1)} %copy-done.25, bf16[8192,64]{0,1:T(8,128)(2,1)} %param.19), kind=kOutput, calls=%fused_computation.223 | convolution fusion | flops 268435456 | bytes 5308416 | tf_op jit(solution)/shard_map/dot_general | solution.py:169
  190.1 1.4 pad_maximum_fusion.5
  191.5 5.1 %fusion.2 = f32[256,1792]{1,0:T(8,128)S(1)} fusion(bf16[8192,1792]{1,0:T(8,128)(2,1)} %param.15, bf16[256,4096]{1,0:T(8,128)(2,1)S(1)} %pad_maximum_fusion.5), kind=kOutput, calls=%fused_computation.2 | convolution fusion | flops 1879048192 | bytes 10223616 | tf_op jit(solution)/shard_map/dot_general | solution.py:158
  196.7 5.2 %fusion = f32[256,1792]{1,0:T(8,128)S(1)} fusion(bf16[8192,1792]{1,0:T(8,128)(2,1)} %param.15, bf16[256,4096]{1,0:T(8,128)(2,1)S(1)} %pad_maximum_fusion.5), kind=kOutput, calls=%fused_computation | convolution fusion | flops 1879048192 | bytes 10223616 | tf_op jit(solution)/shard_map/dot_general | solution.py:158
  201.8 5.1 %fusion.8 = f32[256,1792]{1,0:T(8,128)S(1)} fusion(bf16[8192,1792]{1,0:T(8,128)(2,1)} %param.16, bf16[256,4096]{1,0:T(8,128)(2,1)S(1)} %pad_maximum_fusion.5), kind=kOutput, calls=%fused_computation.8 | convolution fusion | flops 1879048192 | bytes 10223616 | tf_op jit(solution)/shard_map/dot_general | solution.py:158
  207.0 5.1 %fusion.10 = f32[256,1792]{1,0:T(8,128)S(1)} fusion(bf16[8192,1792]{1,0:T(8,128)(2,1)} %param.16, bf16[256,4096]{1,0:T(8,128)(2,1)S(1)} %pad_maximum_fusion.5), kind=kOutput, calls=%fused_computation.10 | convolution fusion | flops 1879048192 | bytes 10223616 | tf_op jit(solution)/shard_map/dot_general | solution.py:158
  212.2 1.5 pad_maximum_fusion.4
  214.1 5.1 %fusion.4 = f32[256,1792]{1,0:T(8,128)S(1)} fusion(bf16[8192,1792]{1,0:T(8,128)(2,1)} %param.15, bf16[256,4096]{1,0:T(8,128)(2,1)S(1)} %pad_maximum_fusion.4), kind=kOutput, calls=%fused_computation.4 | convolution fusion | flops 1879048192 | bytes 10223616 | tf_op jit(solution)/shard_map/dot_general | solution.py:158
  220.2 5.4 %fusion.12 = f32[256,1792]{1,0:T(8,128)S(1)} fusion(bf16[8192,1792]{1,0:T(8,128)(2,1)} %param.16, bf16[256,4096]{1,0:T(8,128)(2,1)S(1)} %pad_maximum_fusion.4), kind=kOutput, calls=%fused_computation.12 | convolution fusion | flops 1879048192 | bytes 10223616 | tf_op jit(solution)/shard_map/dot_general | solution.py:158
  225.8 5.4 %fusion.16 = f32[256,1792]{1,0:T(8,128)S(1)} fusion(bf16[1792,8192]{1,0:T(8,128)(2,1)} %param.17, bf16[256,4096]{1,0:T(8,128)(2,1)S(1)} %pad_maximum_fusion.3), kind=kOutput, calls=%fused_computation.16 | convolution fusion | flops 1879048192 | bytes 10223616 | tf_op jit(solution)/shard_map/dot_general | solution.py:158
  233.4 5.4 %fusion.18 = f32[256,1792]{1,0:T(8,128)S(1)} fusion(bf16[1792,8192]{1,0:T(8,128)(2,1)} %param.17, bf16[256,4096]{1,0:T(8,128)(2,1)S(1)} %pad_maximum_fusion.3), kind=kOutput, calls=%fused_computation.18 | convolution fusion | flops 1879048192 | bytes 10223616 | tf_op jit(solution)/shard_map/dot_general | solution.py:158
  238.8 1.4 pad_maximum_fusion.2
  241.2 5.2 %fusion.20 = f32[256,1792]{1,0:T(8,128)S(1)} fusion(bf16[1792,8192]{1,0:T(8,128)(2,1)} %param.17, bf16[256,4096]{1,0:T(8,128)(2,1)S(1)} %pad_maximum_fusion.2), kind=kOutput, calls=%fused_computation.20 | convolution fusion | flops 1879048192 | bytes 10223616 | tf_op jit(solution)/shard_map/dot_general | solution.py:158
  246.4 5.2 %fusion.36 = f32[256,1792]{1,0:T(8,128)S(1)} fusion(f32[256,1792]{1,0:T(8,128)S(1)} %fusion, f32[256,1792]{1,0:T(8,128)S(1)} %fusion.2, f32[256,1792]{1,0:T(8,128)S(1)} %fusion.4, bf16[8192,1792]{1,0:T(8,128)(2,1)} %param.15, bf16[256,4096]{1,0:T(8,128)(2,1)S(1)} %pad_maximum_fusion.4), kind=kOutput, calls=%fused_computation.28 | convolution fusion | flops 1880424448 | bytes 15728640 | tf_op jit(solution)/shard_map/dot_general | solution.py:158
  251.6 5.2 %fusion.42 = f32[256,1792]{1,0:T(8,128)S(1)} fusion(f32[256,1792]{1,0:T(8,128)S(1)} %fusion.8, f32[256,1792]{1,0:T(8,128)S(1)} %fusion.10, f32[256,1792]{1,0:T(8,128)S(1)} %fusion.12, bf16[8192,1792]{1,0:T(8,128)(2,1)} %param.16, bf16[256,4096]{1,0:T(8,128)(2,1)S(1)} %pad_maximum_fusion.4), kind=kOutput, calls=%fused_computation.30 | convolution fusion | flops 1880424448 | bytes 15728640 | tf_op jit(solution)/shard_map/dot_general | solution.py:158
  257.6 5.3 %fusion.48 = f32[256,1792]{1,0:T(8,128)S(1)} fusion(f32[256,1792]{1,0:T(8,128)S(1)} %fusion.16, f32[256,1792]{1,0:T(8,128)S(1)} %fusion.18, f32[256,1792]{1,0:T(8,128)S(1)} %fusion.20, bf16[1792,8192]{1,0:T(8,128)(2,1)} %param.17, bf16[256,4096]{1,0:T(8,128)(2,1)S(1)} %pad_maximum_fusion.2), kind=kOutput, calls=%fused_computation.32 | convolution fusion | flops 1880424448 | bytes 15728640 | tf_op jit(solution)/shard_map/dot_general | solution.py:158
  263.9 1.3 fusion.73
  266.6 1.4 fusion.56
  271.7 1.6 collective-permute-start.32
  273.3 3.5 %collective-permute-done.27 = f32[3,12,512]{2,1,0:T(8,128)S(1)} collective-permute-done((f32[3,12,512]{2,1,0:T(8,128)S(1)}, f32[3,12,512]{2,1,0:T(8,128)S(1)}, u32[]{:S(2)}, u32[]{:S(2)}) %collective-permute-start.27) | collective-permute-done | bytes 73760 | tf_op jit(solution)/shard_map/ppermute | solution.py:101
  276.8 2.5 collective-permute-start.28
  279.3 1.3 collective-permute-start.30
  280.6 5.6 %collective-permute-start.29 = (f32[12,512]{1,0:T(8,128)S(1)}, f32[12,512]{1,0:T(8,128)S(1)}, u32[]{:S(2)}, u32[]{:S(2)}) collective-permute-start(f32[12,512]{1,0:T(8,128)S(1)} %get-tuple-element.30), channel_id=1, source_target_pairs={{0,8},{1,9},{2,10},{3,11},{8,0},{9,1},{10,2},{11,3},{12,4},{13,5},... | collective-permute-start | bytes 73736 | tf_op jit(solution)/shard_map/ppermute | solution.py:101
  286.5 1.4 collective-permute-start.35
  288.7 9.5 %collective-permute-done.35 = f32[512,64]{1,0:T(8,128)S(1)} collective-permute-done((f32[512,64]{1,0:T(8,128)S(1)}, f32[512,64]{1,0:T(8,128)S(1)}, u32[]{:S(2)}, u32[]{:S(2)}) %collective-permute-start.35) | collective-permute-done | bytes 131104 | tf_op jit(solution)/shard_map/ppermute | solution.py:101
  298.2 3.0 collective-permute-done.34
  301.2 8.3 %collective-permute-done.33 = f32[512,64]{1,0:T(8,128)S(1)} collective-permute-done((f32[512,64]{1,0:T(8,128)S(1)}, f32[512,64]{1,0:T(8,128)S(1)}, u32[]{:S(2)}, u32[]{:S(2)}) %collective-permute-start.33) | collective-permute-done | bytes 131104 | tf_op jit(solution)/shard_map/ppermute | solution.py:101
  312.1 3.2 collective-permute-done.37
  315.3 2.8 collective-permute-start.40
  319.5 4.1 %collective-permute-done.39 = f32[24,8]{1,0:T(8,128)S(1)} collective-permute-done((f32[24,8]{1,0:T(8,128)S(1)}, f32[24,8]{1,0:T(8,128)S(1)}, u32[]{:S(2)}, u32[]{:S(2)}) %collective-permute-start.39) | collective-permute-done | bytes 800 | tf_op jit(solution)/shard_map/ppermute | solution.py:101
  324.2 2.2 shard_map.131
  326.4 1.4 copy.68
  (228 shorter events, 40.5 us)
Async XLA Ops:
  0.6 162.8 %copy-start = (bf16[1792,64]{0,1:T(8,128)(2,1)S(1)}, bf16[1792,64]{0,1:T(8,128)(2,1)}, u32[]{:S(2)}) copy-start(bf16[1792,64]{0,1:T(8,128)(2,1)} %param.20) | copy-start | bytes 688132
  0.6 16.0 %collective-permute-start.6 = (bf16[32,8192]{1,0:T(8,128)(2,1)}, bf16[32,8192]{1,0:T(8,128)(2,1)S(1)}, u32[]{:S(2)}, u32[]{:S(2)}) collective-permute-start(bf16[32,8192]{1,0:T(8,128)(2,1)} %param.12), channel_id=1, source_target_pairs={{0,2},{1,3},{2,0},{3,1},{4,6},{5,7},{6,4},{7,5},{8,10},{9,11},{10,... | collective-permute-start | bytes 1572872 | tf_op jit(solution)/shard_map/ppermute | solution.py:101
  3.7 15.2 %collective-permute-start.5 = (bf16[32,8192]{1,0:T(8,128)(2,1)}, bf16[32,8192]{1,0:T(8,128)(2,1)S(1)}, u32[]{:S(2)}, u32[]{:S(2)}) collective-permute-start(bf16[32,8192]{1,0:T(8,128)(2,1)} %param.12), channel_id=1, source_target_pairs={{0,4},{1,5},{2,6},{3,7},{4,0},{5,1},{6,2},{7,3},{8,12},{9,13},{10,... | collective-permute-start | bytes 1572872 | tf_op jit(solution)/shard_map/ppermute | solution.py:101
  5.3 22.6 %collective-permute-start.1 = (bf16[32,8192]{1,0:T(8,128)(2,1)}, bf16[32,8192]{1,0:T(8,128)(2,1)S(1)}, u32[]{:S(2)}, u32[]{:S(2)}) collective-permute-start(bf16[32,8192]{1,0:T(8,128)(2,1)} %param.13), channel_id=1, source_target_pairs={{0,2},{1,3},{2,0},{3,1},{4,6},{5,7},{6,4},{7,5},{8,10},{9,11},{10,... | collective-permute-start | bytes 1572872 | tf_op jit(solution)/shard_map/ppermute | solution.py:101
  5.8 24.3 %collective-permute-start = (bf16[32,8192]{1,0:T(8,128)(2,1)}, bf16[32,8192]{1,0:T(8,128)(2,1)S(1)}, u32[]{:S(2)}, u32[]{:S(2)}) collective-permute-start(bf16[32,8192]{1,0:T(8,128)(2,1)} %param.13), channel_id=1, source_target_pairs={{0,4},{1,5},{2,6},{3,7},{4,0},{5,1},{6,2},{7,3},{8,12},{9,13},{10,... | collective-permute-start | bytes 1572872 | tf_op jit(solution)/shard_map/ppermute | solution.py:101
  16.7 18.9 %collective-permute-start.7 = (bf16[32,4096]{1,0:T(8,128)(2,1)S(1)}, bf16[32,4096]{1,0:T(8,128)(2,1)S(1)}, u32[]{:S(2)}, u32[]{:S(2)}) collective-permute-start(bf16[32,4096]{1,0:T(8,128)(2,1)S(1)} %slice.202), channel_id=1, source_target_pairs={{0,4},{1,5},{2,6},{3,7},{4,0},{5,1},{6,2},{7,3},{8,12},{9,13},{10,... | collective-permute-start | bytes 786440 | tf_op jit(solution)/shard_map/ppermute | solution.py:101
  18.9 17.5 %collective-permute-start.8 = (bf16[32,4096]{1,0:T(8,128)(2,1)S(1)}, bf16[32,4096]{1,0:T(8,128)(2,1)S(1)}, u32[]{:S(2)}, u32[]{:S(2)}) collective-permute-start(bf16[32,4096]{1,0:T(8,128)(2,1)S(1)} %slice.203), channel_id=1, source_target_pairs={{0,2},{1,3},{2,0},{3,1},{4,6},{5,7},{6,4},{7,5},{8,10},{9,11},{10,... | collective-permute-start | bytes 786440 | tf_op jit(solution)/shard_map/ppermute | solution.py:101
  27.9 12.4 %collective-permute-start.2 = (bf16[32,4096]{1,0:T(8,128)(2,1)S(1)}, bf16[32,4096]{1,0:T(8,128)(2,1)S(1)}, u32[]{:S(2)}, u32[]{:S(2)}) collective-permute-start(bf16[32,4096]{1,0:T(8,128)(2,1)S(1)} %slice.200), channel_id=1, source_target_pairs={{0,4},{1,5},{2,6},{3,7},{4,0},{5,1},{6,2},{7,3},{8,12},{9,13},{10,... | collective-permute-start | bytes 786440 | tf_op jit(solution)/shard_map/ppermute | solution.py:101
  30.1 10.2 %collective-permute-start.3 = (bf16[32,4096]{1,0:T(8,128)(2,1)S(1)}, bf16[32,4096]{1,0:T(8,128)(2,1)S(1)}, u32[]{:S(2)}, u32[]{:S(2)}) collective-permute-start(bf16[32,4096]{1,0:T(8,128)(2,1)S(1)} %slice.201), channel_id=1, source_target_pairs={{0,2},{1,3},{2,0},{3,1},{4,6},{5,7},{6,4},{7,5},{8,10},{9,11},{10,... | collective-permute-start | bytes 786440 | tf_op jit(solution)/shard_map/ppermute | solution.py:101
  33.4 3.7 %copy-start.4 = (bf16[32,8192]{1,0:T(8,128)(2,1)S(1)}, bf16[32,8192]{1,0:T(8,128)(2,1)}, u32[]{:S(2)}) copy-start(bf16[32,8192]{1,0:T(8,128)(2,1)} %param.12) | copy-start | bytes 1572868
  38.8 9.0 %collective-permute-start.18 = (bf16[128,2048]{1,0:T(8,128)(2,1)S(1)}, bf16[128,2048]{1,0:T(8,128)(2,1)S(1)}, u32[]{:S(2)}, u32[]{:S(2)}) collective-permute-start(bf16[128,2048]{1,0:T(8,128)(2,1)S(1)} %get-tuple-element.16), channel_id=1, source_target_pairs={{4,8},{5,9},{6,10},{7,11},{8,4},{9,5},{10,6},{11,7},{20,24},{21,25... | collective-permute-start | bytes 1572872 | tf_op jit(solution)/shard_map/ppermute | solution.py:101
  39.6 9.5 %collective-permute-start.22 = (bf16[128,2048]{1,0:T(8,128)(2,1)S(1)}, bf16[128,2048]{1,0:T(8,128)(2,1)S(1)}, u32[]{:S(2)}, u32[]{:S(2)}) collective-permute-start(bf16[128,2048]{1,0:T(8,128)(2,1)S(1)} %get-tuple-element.17), channel_id=1, source_target_pairs={{4,8},{5,9},{6,10},{7,11},{8,4},{9,5},{10,6},{11,7},{20,24},{21,25... | collective-permute-start | bytes 1572872 | tf_op jit(solution)/shard_map/ppermute | solution.py:101
  43.8 6.8 %copy-start.2 = (bf16[128,8192]{1,0:T(8,128)(2,1)S(1)}, bf16[128,8192]{1,0:T(8,128)(2,1)}, u32[]{:S(2)}) copy-start(bf16[128,8192]{1,0:T(8,128)(2,1)} %copy-done.1) | copy-start | bytes 6291460
  44.8 5.8 %collective-permute-start.10 = (bf16[128,2048]{1,0:T(8,128)(2,1)}, bf16[128,2048]{1,0:T(8,128)(2,1)}, u32[]{:S(2)}, u32[]{:S(2)}) collective-permute-start(bf16[128,2048]{1,0:T(8,128)(2,1)} %get-tuple-element.10), channel_id=1, source_target_pairs={{4,8},{5,9},{6,10},{7,11},{8,4},{9,5},{10,6},{11,7},{20,24},{21,25... | collective-permute-start | bytes 1572872 | tf_op jit(solution)/shard_map/ppermute | solution.py:101
  46.3 4.8 %collective-permute-start.14 = (bf16[128,2048]{1,0:T(8,128)(2,1)}, bf16[128,2048]{1,0:T(8,128)(2,1)}, u32[]{:S(2)}, u32[]{:S(2)}) collective-permute-start(bf16[128,2048]{1,0:T(8,128)(2,1)} %get-tuple-element.11), channel_id=1, source_target_pairs={{4,8},{5,9},{6,10},{7,11},{8,4},{9,5},{10,6},{11,7},{20,24},{21,25... | collective-permute-start | bytes 1572872 | tf_op jit(solution)/shard_map/ppermute | solution.py:101
  47.8 21.6 %collective-permute-start.19 = (bf16[128,2048]{1,0:T(8,128)(2,1)S(1)}, bf16[128,2048]{1,0:T(8,128)(2,1)}, u32[]{:S(2)}, u32[]{:S(2)}) collective-permute-start(bf16[128,2048]{1,0:T(8,128)(2,1)S(1)} %collective-permute-done.18), channel_id=1, source_target_pairs={{4,0},{5,1},{6,2},{7,3},{8,12},{9,13},{10,14},{11,15},{20,16},{21,... | collective-permute-start | bytes 1572872 | tf_op jit(solution)/shard_map/ppermute | solution.py:101
  49.1 28.4 %collective-permute-start.23 = (bf16[128,2048]{1,0:T(8,128)(2,1)S(1)}, bf16[128,2048]{1,0:T(8,128)(2,1)}, u32[]{:S(2)}, u32[]{:S(2)}) collective-permute-start(bf16[128,2048]{1,0:T(8,128)(2,1)S(1)} %collective-permute-done.22), channel_id=1, source_target_pairs={{4,0},{5,1},{6,2},{7,3},{8,12},{9,13},{10,14},{11,15},{20,16},{21,... | collective-permute-start | bytes 1572872 | tf_op jit(solution)/shard_map/ppermute | solution.py:101
  50.5 83.9 %collective-permute-start.9 = (bf16[128,8192]{1,0:T(8,128)(2,1)S(1)}, bf16[128,8192]{1,0:T(8,128)(2,1)S(1)}, u32[]{:S(2)}, u32[]{:S(2)}) collective-permute-start(bf16[128,8192]{1,0:T(8,128)(2,1)S(1)} %copy-done.2), channel_id=1, source_target_pairs={{0,1},{1,0},{2,3},{3,2},{4,5},{5,4},{6,7},{7,6},{8,9},{9,8},{10,11... | collective-permute-start | bytes 6291464 | tf_op jit(solution)/shard_map/ppermute | solution.py:101
  50.6 114.8 %collective-permute-start.4 = (bf16[128,8192]{1,0:T(8,128)(2,1)}, bf16[128,8192]{1,0:T(8,128)(2,1)S(1)}, u32[]{:S(2)}, u32[]{:S(2)}) collective-permute-start(bf16[128,8192]{1,0:T(8,128)(2,1)} %copy-done.3), channel_id=1, source_target_pairs={{0,1},{1,0},{2,3},{3,2},{4,5},{5,4},{6,7},{7,6},{8,9},{9,8},{10,11... | collective-permute-start | bytes 6291464 | tf_op jit(solution)/shard_map/ppermute | solution.py:101
  51.1 50.4 %collective-permute-start.11 = (bf16[128,2048]{1,0:T(8,128)(2,1)}, bf16[128,2048]{1,0:T(8,128)(2,1)S(1)}, u32[]{:S(2)}, u32[]{:S(2)}) collective-permute-start(bf16[128,2048]{1,0:T(8,128)(2,1)} %collective-permute-done.10), channel_id=1, source_target_pairs={{4,0},{5,1},{6,2},{7,3},{8,12},{9,13},{10,14},{11,15},{20,16},{21,... | collective-permute-start | bytes 1572872 | tf_op jit(solution)/shard_map/ppermute | solution.py:101
  69.4 38.8 %collective-permute-start.15 = (bf16[128,2048]{1,0:T(8,128)(2,1)}, bf16[128,2048]{1,0:T(8,128)(2,1)S(1)}, u32[]{:S(2)}, u32[]{:S(2)}) collective-permute-start(bf16[128,2048]{1,0:T(8,128)(2,1)} %collective-permute-done.14), channel_id=1, source_target_pairs={{4,0},{5,1},{6,2},{7,3},{8,12},{9,13},{10,14},{11,15},{20,16},{21,... | collective-permute-start | bytes 1572872 | tf_op jit(solution)/shard_map/ppermute | solution.py:101
  77.5 31.3 %collective-permute-start.20 = (bf16[128,2048]{1,0:T(8,128)(2,1)S(1)}, bf16[128,2048]{1,0:T(8,128)(2,1)S(1)}, u32[]{:S(2)}, u32[]{:S(2)}) collective-permute-start(bf16[128,2048]{1,0:T(8,128)(2,1)S(1)} %broadcast_select_fusion.1), channel_id=1, source_target_pairs={{0,2},{1,3},{2,0},{3,1},{4,6},{5,7},{6,4},{7,5},{8,10},{9,11},{10,... | collective-permute-start | bytes 1572872 | tf_op jit(solution)/shard_map/ppermute | solution.py:101
  101.5 13.4 %collective-permute-start.24 = (bf16[128,2048]{1,0:T(8,128)(2,1)S(1)}, bf16[128,2048]{1,0:T(8,128)(2,1)S(1)}, u32[]{:S(2)}, u32[]{:S(2)}) collective-permute-start(bf16[128,2048]{1,0:T(8,128)(2,1)S(1)} %broadcast_select_fusion), channel_id=1, source_target_pairs={{0,2},{1,3},{2,0},{3,1},{4,6},{5,7},{6,4},{7,5},{8,10},{9,11},{10,... | collective-permute-start | bytes 1572872 | tf_op jit(solution)/shard_map/ppermute | solution.py:101
  108.2 18.0 %collective-permute-start.12 = (bf16[128,2048]{1,0:T(8,128)(2,1)S(1)}, bf16[128,2048]{1,0:T(8,128)(2,1)S(1)}, u32[]{:S(2)}, u32[]{:S(2)}) collective-permute-start(bf16[128,2048]{1,0:T(8,128)(2,1)S(1)} %broadcast_select_fusion.3), channel_id=1, source_target_pairs={{0,2},{1,3},{2,0},{3,1},{4,6},{5,7},{6,4},{7,5},{8,10},{9,11},{10,... | collective-permute-start | bytes 1572872 | tf_op jit(solution)/shard_map/ppermute | solution.py:101
  108.8 24.3 %collective-permute-start.16 = (bf16[128,2048]{1,0:T(8,128)(2,1)S(1)}, bf16[128,2048]{1,0:T(8,128)(2,1)S(1)}, u32[]{:S(2)}, u32[]{:S(2)}) collective-permute-start(bf16[128,2048]{1,0:T(8,128)(2,1)S(1)} %broadcast_select_fusion.2), channel_id=1, source_target_pairs={{0,2},{1,3},{2,0},{3,1},{4,6},{5,7},{6,4},{7,5},{8,10},{9,11},{10,... | collective-permute-start | bytes 1572872 | tf_op jit(solution)/shard_map/ppermute | solution.py:101
  114.9 97.2 %collective-permute-start.21 = (bf16[128,4096]{1,0:T(8,128)(2,1)}, bf16[128,4096]{1,0:T(8,128)(2,1)}, u32[]{:S(2)}, u32[]{:S(2)}) collective-permute-start(bf16[128,4096]{1,0:T(8,128)(2,1)} %pad_maximum_fusion.12), channel_id=1, source_target_pairs={{0,1},{1,0},{2,3},{3,2},{4,5},{5,4},{6,7},{7,6},{8,9},{9,8},{10,11... | collective-permute-start | bytes 3145736 | tf_op jit(solution)/shard_map/ppermute | solution.py:101
  115.0 11.2 %copy-start.10 = (bf16[128,2048]{1,0:T(8,128)(2,1)}, bf16[128,2048]{1,0:T(8,128)(2,1)S(1)}, u32[]{:S(2)}) copy-start(bf16[128,2048]{1,0:T(8,128)(2,1)S(1)} %get-tuple-element.18) | copy-start | bytes 1572868
  115.0 11.2 %copy-start.12 = (bf16[128,2048]{1,0:T(8,128)(2,1)}, bf16[128,2048]{1,0:T(8,128)(2,1)S(1)}, u32[]{:S(2)}) copy-start(bf16[128,2048]{1,0:T(8,128)(2,1)S(1)} %get-tuple-element.19) | copy-start | bytes 1572868
  126.2 63.9 %collective-permute-start.25 = (bf16[128,4096]{1,0:T(8,128)(2,1)}, bf16[128,4096]{1,0:T(8,128)(2,1)}, u32[]{:S(2)}, u32[]{:S(2)}) collective-permute-start(bf16[128,4096]{1,0:T(8,128)(2,1)} %pad_maximum_fusion.13), channel_id=1, source_target_pairs={{0,1},{1,0},{2,3},{3,2},{4,5},{5,4},{6,7},{7,6},{8,9},{9,8},{10,11... | collective-permute-start | bytes 3145736 | tf_op jit(solution)/shard_map/ppermute | solution.py:101
  126.2 7.0 %copy-start.6 = (bf16[128,2048]{1,0:T(8,128)(2,1)}, bf16[128,2048]{1,0:T(8,128)(2,1)S(1)}, u32[]{:S(2)}) copy-start(bf16[128,2048]{1,0:T(8,128)(2,1)S(1)} %get-tuple-element.8) | copy-start | bytes 1572868
  126.3 7.0 %copy-start.8 = (bf16[128,2048]{1,0:T(8,128)(2,1)}, bf16[128,2048]{1,0:T(8,128)(2,1)S(1)}, u32[]{:S(2)}) copy-start(bf16[128,2048]{1,0:T(8,128)(2,1)S(1)} %get-tuple-element.9) | copy-start | bytes 1572868
  127.4 7.5 %copy-start.22 = (bf16[256,8192]{1,0:T(8,128)(2,1)S(1)}, bf16[256,8192]{1,0:T(8,128)(2,1)}, u32[]{:S(2)}) copy-start(bf16[256,8192]{1,0:T(8,128)(2,1)} %get-tuple-element.24) | copy-start | bytes 12582916
  133.1 105.6 %collective-permute-start.13 = (bf16[128,4096]{1,0:T(8,128)(2,1)}, bf16[128,4096]{1,0:T(8,128)(2,1)}, u32[]{:S(2)}, u32[]{:S(2)}) collective-permute-start(bf16[128,4096]{1,0:T(8,128)(2,1)} %pad_maximum_fusion.10), channel_id=1, source_target_pairs={{0,1},{1,0},{2,3},{3,2},{4,5},{5,4},{6,7},{7,6},{8,9},{9,8},{10,11... | collective-permute-start | bytes 3145736 | tf_op jit(solution)/shard_map/ppermute | solution.py:101
  134.4 91.2 %collective-permute-start.17 = (bf16[128,4096]{1,0:T(8,128)(2,1)}, bf16[128,4096]{1,0:T(8,128)(2,1)S(1)}, u32[]{:S(2)}, u32[]{:S(2)}) collective-permute-start(bf16[128,4096]{1,0:T(8,128)(2,1)} %pad_maximum_fusion.11), channel_id=1, source_target_pairs={{0,1},{1,0},{2,3},{3,2},{4,5},{5,4},{6,7},{7,6},{8,9},{9,8},{10,11... | collective-permute-start | bytes 3145736 | tf_op jit(solution)/shard_map/ppermute | solution.py:101
  148.7 13.5 %copy-start.27 = (bf16[8192,64]{0,1:T(8,128)(2,1)S(1)}, bf16[8192,64]{0,1:T(8,128)(2,1)}, u32[]{:S(2)}) copy-start(bf16[8192,64]{0,1:T(8,128)(2,1)} %param.18) | copy-start | bytes 3145732
  165.9 16.3 %copy-start.25 = (bf16[256,8192]{1,0:T(8,128)(2,1)}, bf16[256,8192]{1,0:T(8,128)(2,1)S(1)}, u32[]{:S(2)}) copy-start(bf16[256,8192]{1,0:T(8,128)(2,1)S(1)} %constant_dynamic-update-slice_fusion.2) | copy-start | bytes 12582916
  165.9 16.3 %copy-start.30 = (bf16[1792,64]{0,1:T(8,128)(2,1)S(1)}, bf16[1792,64]{0,1:T(8,128)(2,1)}, u32[]{:S(2)}) copy-start(bf16[1792,64]{0,1:T(8,128)(2,1)} %param.22) | copy-start | bytes 688132
  182.2 2.5 copy-start.32
  186.2 3.9 %copy-start.11 = (bf16[128,2048]{1,0:T(8,128)(2,1)S(1)}, bf16[128,2048]{1,0:T(8,128)(2,1)}, u32[]{:S(2)}) copy-start(bf16[128,2048]{1,0:T(8,128)(2,1)} %copy-done.10) | copy-start | bytes 1572868
  186.2 3.9 %copy-start.13 = (bf16[128,2048]{1,0:T(8,128)(2,1)S(1)}, bf16[128,2048]{1,0:T(8,128)(2,1)}, u32[]{:S(2)}) copy-start(bf16[128,2048]{1,0:T(8,128)(2,1)} %copy-done.12) | copy-start | bytes 1572868
  220.2 5.5 %copy-start.15 = (bf16[128,2048]{1,0:T(8,128)(2,1)S(1)}, bf16[128,2048]{1,0:T(8,128)(2,1)}, u32[]{:S(2)}) copy-start(bf16[128,2048]{1,0:T(8,128)(2,1)} %copy-done.14) | copy-start | bytes 1572868
  220.2 5.5 %copy-start.17 = (bf16[128,2048]{1,0:T(8,128)(2,1)S(1)}, bf16[128,2048]{1,0:T(8,128)(2,1)}, u32[]{:S(2)}) copy-start(bf16[128,2048]{1,0:T(8,128)(2,1)} %copy-done.16) | copy-start | bytes 1572868
  225.8 5.4 %copy-start.29 = (bf16[8192,64]{0,1:T(8,128)(2,1)S(1)}, bf16[8192,64]{0,1:T(8,128)(2,1)}, u32[]{:S(2)}) copy-start(bf16[8192,64]{0,1:T(8,128)(2,1)} %param.19) | copy-start | bytes 3145732
  233.4 5.4 %copy-start.7 = (bf16[128,2048]{1,0:T(8,128)(2,1)S(1)}, bf16[128,2048]{1,0:T(8,128)(2,1)}, u32[]{:S(2)}) copy-start(bf16[128,2048]{1,0:T(8,128)(2,1)} %copy-done.6) | copy-start | bytes 1572868
  233.4 5.4 %copy-start.9 = (bf16[128,2048]{1,0:T(8,128)(2,1)S(1)}, bf16[128,2048]{1,0:T(8,128)(2,1)}, u32[]{:S(2)}) copy-start(bf16[128,2048]{1,0:T(8,128)(2,1)} %copy-done.8) | copy-start | bytes 1572868
  257.6 5.3 %copy-start.31 = (bf16[1792,64]{0,1:T(8,128)(2,1)S(1)}, bf16[1792,64]{0,1:T(8,128)(2,1)}, u32[]{:S(2)}) copy-start(bf16[1792,64]{0,1:T(8,128)(2,1)} %param.22) | copy-start | bytes 688132
  266.2 2.9 copy-start.18
  266.3 5.4 %collective-permute-start.31 = (f32[512,64]{1,0:T(8,128)S(1)}, f32[512,64]{1,0:T(8,128)S(1)}, u32[]{:S(2)}, u32[]{:S(2)}) collective-permute-start(f32[512,64]{1,0:T(8,128)S(1)} %bitcast.110), channel_id=1, source_target_pairs={{0,1},{1,0},{2,3},{3,2},{4,5},{5,4},{6,7},{7,6},{8,9},{9,8},{10,11... | collective-permute-start | bytes 393224 | tf_op jit(solution)/shard_map/ppermute | solution.py:101
  269.5 1.5 collective-permute-start.26
  271.1 5.7 %collective-permute-start.27 = (f32[3,12,512]{2,1,0:T(8,128)S(1)}, f32[3,12,512]{2,1,0:T(8,128)S(1)}, u32[]{:S(2)}, u32[]{:S(2)}) collective-permute-start(f32[3,12,512]{2,1,0:T(8,128)S(1)} %select_bitcast_fusion.1), channel_id=1, source_target_pairs={{0,2},{1,3},{2,0},{3,1},{4,6},{5,7},{6,4},{7,5},{8,10},{9,11},{10,... | collective-permute-start | bytes 221192 | tf_op jit(solution)/shard_map/ppermute | solution.py:101
  271.7 14.8 %collective-permute-start.32 = (f32[512,64]{1,0:T(8,128)S(1)}, f32[512,64]{1,0:T(8,128)S(1)}, u32[]{:S(2)}, u32[]{:S(2)}) collective-permute-start(f32[512,64]{1,0:T(8,128)S(1)} %bitcast_add_fusion.1), channel_id=1, source_target_pairs={{0,2},{1,3},{2,0},{3,1},{4,6},{5,7},{6,4},{7,5},{8,10},{9,11},{10,... | collective-permute-start | bytes 393224 | tf_op jit(solution)/shard_map/ppermute | solution.py:101
  276.8 11.8 %collective-permute-start.28 = (f32[12,512]{1,0:T(8,128)S(1)}, f32[12,512]{1,0:T(8,128)S(1)}, u32[]{:S(2)}, u32[]{:S(2)}) collective-permute-start(f32[12,512]{1,0:T(8,128)S(1)} %get-tuple-element.28), channel_id=1, source_target_pairs={{0,4},{1,5},{2,6},{3,7},{4,8},{5,9},{6,10},{7,11},{12,0},{13,1},{1... | collective-permute-start | bytes 73736 | tf_op jit(solution)/shard_map/ppermute | solution.py:101
  279.3 9.3 %collective-permute-start.30 = (f32[12,512]{1,0:T(8,128)S(1)}, f32[12,512]{1,0:T(8,128)S(1)}, u32[]{:S(2)}, u32[]{:S(2)}) collective-permute-start(f32[12,512]{1,0:T(8,128)S(1)} %get-tuple-element.29), channel_id=1, source_target_pairs={{4,0},{5,1},{6,2},{7,3},{8,4},{9,5},{10,6},{11,7},{12,8},{13,9},{1... | collective-permute-start | bytes 73736 | tf_op jit(solution)/shard_map/ppermute | solution.py:101
  280.6 8.0 %collective-permute-start.29 = (f32[12,512]{1,0:T(8,128)S(1)}, f32[12,512]{1,0:T(8,128)S(1)}, u32[]{:S(2)}, u32[]{:S(2)}) collective-permute-start(f32[12,512]{1,0:T(8,128)S(1)} %get-tuple-element.30), channel_id=1, source_target_pairs={{0,8},{1,9},{2,10},{3,11},{8,0},{9,1},{10,2},{11,3},{12,4},{13,5},... | collective-permute-start | bytes 73736 | tf_op jit(solution)/shard_map/ppermute | solution.py:101
  286.3 23.9 %copy-start.26 = (f32[16,768]{1,0:T(8,128)S(1)}, f32[16,768]{1,0:T(8,128)}, u32[]{:S(2)}) copy-start(f32[16,768]{1,0:T(8,128)} %param.23) | copy-start | bytes 147460
  286.5 11.7 %collective-permute-start.35 = (f32[512,64]{1,0:T(8,128)S(1)}, f32[512,64]{1,0:T(8,128)S(1)}, u32[]{:S(2)}, u32[]{:S(2)}) collective-permute-start(f32[512,64]{1,0:T(8,128)S(1)} %add.203), channel_id=1, source_target_pairs={{0,12},{1,13},{2,14},{3,15},{4,0},{5,1},{6,2},{7,3},{8,4},{9,5},{1... | collective-permute-start | bytes 393224 | tf_op jit(solution)/shard_map/ppermute | solution.py:101
  287.9 13.3 %collective-permute-start.34 = (f32[512,64]{1,0:T(8,128)S(1)}, f32[512,64]{1,0:T(8,128)S(1)}, u32[]{:S(2)}, u32[]{:S(2)}) collective-permute-start(f32[512,64]{1,0:T(8,128)S(1)} %add.203), channel_id=1, source_target_pairs={{0,4},{1,5},{2,6},{3,7},{4,8},{5,9},{6,10},{7,11},{8,12},{9,13},{1... | collective-permute-start | bytes 393224 | tf_op jit(solution)/shard_map/ppermute | solution.py:101
  288.6 20.9 %collective-permute-start.33 = (f32[512,64]{1,0:T(8,128)S(1)}, f32[512,64]{1,0:T(8,128)S(1)}, u32[]{:S(2)}, u32[]{:S(2)}) collective-permute-start(f32[512,64]{1,0:T(8,128)S(1)} %add.203), channel_id=1, source_target_pairs={{0,8},{1,9},{2,10},{3,11},{4,12},{5,13},{6,14},{7,15},{8,0},{9,1},... | collective-permute-start | bytes 393224 | tf_op jit(solution)/shard_map/ppermute | solution.py:101
  310.2 17.5 %copy-start.21 = (f32[8,768]{1,0:T(8,128)}, f32[8,768]{1,0:T(8,128)S(1)}, u32[]{:S(2)}) copy-start(f32[8,768]{1,0:T(8,128)S(1)} %reshape.123) | copy-start | bytes 73732
  310.4 1.2 collective-permute-start.36
  311.6 3.7 %collective-permute-start.37 = (f32[24,8]{1,0:T(8,128)S(1)}, f32[24,8]{1,0:T(8,128)S(1)}, u32[]{:S(2)}, u32[]{:S(2)}) collective-permute-start(f32[24,8]{1,0:T(8,128)S(1)} %add.207), channel_id=1, source_target_pairs={{0,2},{1,3},{2,0},{3,1},{4,6},{5,7},{6,4},{7,5},{8,10},{9,11},{10,... | collective-permute-start | bytes 2312 | tf_op jit(solution)/shard_map/ppermute | solution.py:101
  315.3 4.2 %collective-permute-start.40 = (f32[24,8]{1,0:T(8,128)S(1)}, f32[24,8]{1,0:T(8,128)S(1)}, u32[]{:S(2)}, u32[]{:S(2)}) collective-permute-start(f32[24,8]{1,0:T(8,128)S(1)} %add.208), channel_id=1, source_target_pairs={{0,12},{1,13},{2,14},{3,15},{4,0},{5,1},{6,2},{7,3},{8,4},{9,5},{1... | collective-permute-start | bytes 2312 | tf_op jit(solution)/shard_map/ppermute | solution.py:101
  318.1 5.5 %collective-permute-start.39 = (f32[24,8]{1,0:T(8,128)S(1)}, f32[24,8]{1,0:T(8,128)S(1)}, u32[]{:S(2)}, u32[]{:S(2)}) collective-permute-start(f32[24,8]{1,0:T(8,128)S(1)} %add.208), channel_id=1, source_target_pairs={{0,4},{1,5},{2,6},{3,7},{4,8},{5,9},{6,10},{7,11},{8,12},{9,13},{1... | collective-permute-start | bytes 2312 | tf_op jit(solution)/shard_map/ppermute | solution.py:101
  318.1 5.5 %collective-permute-start.38 = (f32[24,8]{1,0:T(8,128)S(1)}, f32[24,8]{1,0:T(8,128)S(1)}, u32[]{:S(2)}, u32[]{:S(2)}) collective-permute-start(f32[24,8]{1,0:T(8,128)S(1)} %add.208), channel_id=1, source_target_pairs={{0,8},{1,9},{2,10},{3,11},{4,12},{5,13},{6,14},{7,15},{8,0},{9,1},... | collective-permute-start | bytes 2312 | tf_op jit(solution)/shard_map/ppermute | solution.py:101
  (15 other events, 21.2 us)
